TPU v7x, 32 devices: a whole 2x2x4 slice. The times are simulated.
32 devices in a mesh: dp: 8 (over z, y), tensor: 4 (over x, core).
Axes of the slice: x: 2, y: 2, z: 4, core: 2. Of those that a mesh axis runs over, the one named last changes fastest.
Arguments:
- inputs: float32 [16384, 768], P('dp'), may hold values from -6 to 6
- segment_ids: int32 [32, 512], P('dp'), may hold values from 0 to 7, never falling along the last dimension, each value on 1 to 128 neighbouring positions
- w_qkv: float32 [3, 768, 768], P(None, None, 'tensor')
- b_qv: float32 [2, 768], P(None, 'tensor'), may hold values from -3 to 3
- w_out: float32 [768, 768], P('tensor')
- w_ff1: float32 [768, 3072], P(None, 'tensor')
- b_ff1: float32 [3072], P('tensor'), may hold values from -3 to 3
- w_ff2: float32 [3072, 768], P('tensor')
- norm_gains: float32 [2, 768], replicated, may hold values from 0.25 to 1.75
- shift_biases: float32 [4, 768], replicated, may hold values from -2 to 2
- act_ranges: float32 [4], replicated, may hold values from 1 to 24
- cotangent: float32 [16384, 768], P('dp'), may hold values from -6 to 6
Outputs:
- layer_out: float32 [16384, 768], P('dp')
- input_grad: float32 [16384, 768], P('dp')
- grad_qkv: float32 [3, 768, 768], P(None, None, 'tensor')
- grad_bqv: float32 [2, 768], P(None, 'tensor')
- grad_out: float32 [768, 768], P('tensor')
- grad_ff1: float32 [768, 3072], P(None, 'tensor')
- grad_bff1: float32 [3072], P('tensor')
- grad_ff2: float32 [3072, 768], P('tensor')
- grad_gains: float32 [2, 768], P(None, 'tensor')
- grad_shifts: float32 [4, 768], P(None, 'tensor')
- weight_max: float32 [6], replicated
Inputs may be any that keep to these rules, and one draw needn't show every extreme that they name: `segment_ids`: equal ids within a packed row mark one example; ids never fall along a row.
All inputs are finite; a program needn't handle non-finite values.
Results may differ from a plain program's by a relative error of at most 0.019.
Values may be sent and summed in bfloat16 or wider, within the bound.
A program may use at most 192 MiB of HBM per device.

v0:
```python
import functools
import math

import jax
import jax.numpy as jnp
from jax import lax
from jax.experimental import pallas as pl
from jax.experimental.pallas import tpu as pltpu
from jax.sharding import PartitionSpec as P

HD = 64
SPAN = 128
QB = 256
MASKED = -1e30
EPSILON = 1e-06
ROOT_HALF = 0.7071067811865476
INV_ROOT_TWO_PI = 0.3989422804014327
STAIR = (
    6.579734980213376,
    -12.987641368031495,
    12.20087719668052,
    -6.61489684889321,
    2.04264519055443,
)
MIB = 1 << 20
MESH = pl.DeviceIdType.MESH
F32 = jnp.float32
BF16 = jnp.bfloat16
ANY = pl.BlockSpec(memory_space=pl.ANY)
VMEM = pl.BlockSpec(memory_space=pltpu.VMEM)
SMEM = pl.BlockSpec(memory_space=pltpu.SMEM)
S = jax.ShapeDtypeStruct


def flip(value, bit):
    return value + bit - 2 * bit * ((value // bit) % 2)


def dot_nn(left, right):
    return lax.dot_general(left, right, (((1,), (0,)), ((), ())), preferred_element_type=F32)


def dot_nt(left, right):
    return lax.dot_general(left, right, (((1,), (1,)), ((), ())), preferred_element_type=F32)


def dot_tn(left, right):
    return lax.dot_general(left, right, (((0,), (0,)), ((), ())), preferred_element_type=F32)


def stairs(levels):
    whole = jnp.round(levels)
    rest = levels - whole
    square = rest * rest
    curve = STAIR[4]
    for factor in STAIR[3::-1]:
        curve = curve * square + factor
    return whole + rest * square * curve


def quantize(values, bound):
    squash = jnp.tanh(values * (1.0 / bound))
    return stairs(127.0 * squash) * (bound / 127.0), squash


def norm(hidden):
    centred = hidden - jnp.mean(hidden, -1, keepdims=True)
    inverse = lax.rsqrt(jnp.mean(centred * centred, -1, keepdims=True) + EPSILON)
    return centred * inverse, inverse


def norm_back(scaled, normed, inverse):
    return inverse * (
        scaled
        - jnp.mean(scaled, -1, keepdims=True)
        - normed * jnp.mean(scaled * normed, -1, keepdims=True)
    )


def windows(length):
    found = []
    for first in range(0, length, QB):
        low = max(0, first - SPAN)
        found.append((first, low, min(length, first + QB + SPAN) - low))
    return found


DIRECT = (0, 1, 2, 3, 11)


def forward_kernel(
    wqkv, wout, wff1, wff2, bqv, bff1, x_hbm, cot_hbm, seg_ref, gains, shifts, ranges,
    bank_out, top_out, xq_out, xs_out, q_out, k_out, v_out, p_out, cq_out, cs_out, nq_out, xh_out,
    inv_out, lo_out, gq_out, factor_out, dh2_out, do_out, sums_out,
    bank, flat, x, xq, xs, qkv, probs, cq, cs, total, bias, xh, nq, inv, small, scales,
    sem, out_sem, p_sem, end_sem, lo_s, lo_r, small_s, small_r, sib_s, sib_r, far_s, far_r,
    direct_s, direct_r, side_s, side_r, inner_s, inner_r, last_s, last_r, pass_s, pass_r,
):
    t, d = lax.axis_index("tensor"), lax.axis_index("dp")
    c, pair, corner = t % 2, t // 2, d % 4
    sib, far, side, inner = (d, flip(t, 1)), (d, flip(t, 2)), (flip(d, 1), t), (flip(d, 2), t)
    diagonal = (d, flip(flip(t, 1), 2))
    cols, width = wout.shape
    hidden = wff1.shape[1]
    tokens = x.shape[0]
    length = seg_ref.shape[1]
    rows_here = tokens // length
    lanes_half = width // 2
    wins = windows(length)
    size = wins[0][2]
    blocks = tokens // QB
    heads = width // 256
    units = rows_here * heads
    piece = cols
    pieces = bank.shape[1] // piece
    quarter = piece // 4

    def load(i, src, dst):
        copy = pltpu.make_async_copy(src, dst, sem.at[i])
        copy.start()
        return copy

    mine = pl.ds(pl.multiple_of(c * tokens, QB), tokens)
    feed_1, feed_2 = 4 * cols, 4 * cols + width
    loads = [load(j, wqkv.at[j], flat.at[j * cols : (j + 1) * cols]) for j in range(3)]
    loads.append(load(3, wout, flat.at[3 * cols : feed_1]))
    loads.append(load(4, wff1, flat.at[feed_1:feed_2]))
    spans = [(j * cols, cols) for j in range(4)]
    spans += [(4 * cols, width), (4 * cols + width, hidden)]

    barrier = pltpu.get_barrier_semaphore()
    for peer in (sib, far, diagonal, side, inner):
        pl.semaphore_signal(barrier, inc=1, device_id=peer, device_id_type=MESH)
    small[pl.ds(t, 1)] = jnp.zeros((1, 8, width), F32)
    small[pl.ds(t, 1), 0:1, 0:hidden] = bff1[...].reshape(1, 1, hidden)
    small[pl.ds(t, 1), 1:3, 0:cols] = bqv[...][None]
    for j, (begin, count) in enumerate(spans):
        loads[j].wait()
        if j == 3:
            loads.append(load(5, wff2, flat.at[feed_2 : feed_2 + hidden]))
        if j == 4:
            x_load = load(6, x_hbm.at[mine], x)
        top = jnp.max(jnp.abs(flat[begin : begin + count]), axis=(0, 1), keepdims=True)
        small[pl.ds(t, 1), 3:4, 128 * j : 128 * (j + 1)] = jnp.broadcast_to(top, (1, 128))[None]
    pl.semaphore_wait(barrier, 5)
    sends = []
    for i, peer in enumerate((sib, far, diagonal)):
        copy = pltpu.make_async_remote_copy(
            src_ref=small.at[t], dst_ref=small.at[t], send_sem=small_s.at[i],
            recv_sem=small_r.at[i], device_id=peer, device_id_type=MESH,
        )
        copy.start()
        sends.append(copy)

    x_load.wait()

    def input_block(b, _):
        rows = pl.ds(pl.multiple_of(b * QB, QB), QB)
        coded, squash = quantize(x[rows], ranges[0])
        xq[rows] = coded.astype(BF16)
        xs[rows] = (1.0 - squash * squash).astype(BF16)
        return 0

    lax.fori_loop(0, blocks, input_block, 0)
    for r in range(rows_here):
        seg = jnp.broadcast_to(seg_ref[pl.ds(c * rows_here + r, 1)], (16, length))
        hot = (lax.broadcasted_iota(jnp.int32, (16, length), 0) == seg).astype(F32).astype(BF16)
        for b, (first, low, _) in enumerate(wins):
            same = dot_tn(hot[:, first : first + QB], hot[:, low : low + size])
            bias[r, b] = (same - 1.0) * -MASKED
    outs = []

    def put(src, dst):
        copy = pltpu.make_async_copy(src, dst, out_sem.at[len(outs)])
        copy.start()
        outs.append(copy)
        return copy

    for copy in sends:
        copy.wait()
    top_row = jnp.max(small[:, 3:4, :], axis=0)
    for j in range(len(spans)):
        top_out[j] = jnp.max(top_row[:, 128 * j : 128 * (j + 1)])

    other = flip(t, 2)
    next_side, next_inner, across = flip(corner, 1), flip(corner, 2), flip(flip(corner, 1), 2)

    def moved(p, shard, which, sems, at, to):
        rows = pl.ds(pl.multiple_of(p * piece + which * quarter, 16), quarter)
        there = bank.at[shard, rows]
        return pltpu.make_async_remote_copy(
            src_ref=there, dst_ref=there, send_sem=sems[0].at[at], recv_sem=sems[1].at[at],
            device_id=to, device_id_type=MESH,
        )

    def sib_copy(p):
        there = bank.at[t, pl.ds(pl.multiple_of(p * piece, 16), piece)]
        return pltpu.make_async_remote_copy(
            src_ref=there, dst_ref=there, send_sem=sib_s.at[p], recv_sem=sib_r.at[p],
            device_id=sib, device_id_type=MESH,
        )

    far_copy = lambda p: moved(p, t, corner, (far_s, far_r), p, far)
    direct_copy = lambda p: moved(p, t, across, (direct_s, direct_r), p, far)
    side_copy = lambda p: moved(p, other, corner, (side_s, side_r), p, side)
    inner_copy = lambda p: moved(p, other, corner, (inner_s, inner_r), p, inner)

    def last_copy(p):
        if p % 2 == 0:
            return moved(p, other, next_inner, (last_s, last_r), p, side)
        return moved(p, other, next_side, (last_s, last_r), p, inner)

    def pass_copy(k, p):
        which = (corner, next_side, next_inner, across)[k]
        return moved(p, other, which, (pass_s, pass_r), (k, p), sib)

    for j in range(len(spans)):
        top = jnp.concatenate([top_row[:, 128 * j : 128 * (j + 1)]] * (width // 128), axis=1)
        scales[0, j : j + 1] = 127.0 / top
        scales[1, j : j + 1] = top / 127.0
    per_feed = width // piece

    def code(p, _):
        at = pl.ds(pl.multiple_of(p * piece, 16), piece)
        late = jnp.maximum(p - 4, 0)
        which = pl.ds(jnp.minimum(p, 4) + late // per_feed, 1)
        bank[t, at] = (stairs(flat[at] * scales[0, which]) * scales[1, which]).astype(BF16)
        far_copy(p).start()
        sib_copy(p).start()

        @pl.when(p == 2)
        def _():
            for first in range(3):
                direct_copy(first).start()

        pl.when(p == 3)(lambda: direct_copy(3).start())
        pl.when(p == pieces - 1)(lambda: direct_copy(pieces - 1).start())
        return 0

    lax.fori_loop(0, pieces, code, 0)
    xq_put = put(xq, xq_out)
    put(xs, xs_out)
    put(bank.at[t], bank_out.at[t])

    def far_step(*found):
        for p in found:
            far_copy(p).wait_recv()
            side_copy(p).start()
            inner_copy(p).start()
            pass_copy(0, p).start()

    def side_step(*found):
        for p in found:
            side_copy(p).wait_recv()
            if p not in DIRECT and p % 2 == 1:
                last_copy(p).start()
            pass_copy(1, p).start()
            inner_copy(p).wait_recv()
            if p not in DIRECT and p % 2 == 0:
                last_copy(p).start()
            pass_copy(2, p).start()

    def last_step(*found):
        for p in found:
            (direct_copy(p) if p in DIRECT else last_copy(p)).wait_recv()
            pass_copy(3, p).start()

    def arrived(own, p):
        if own:
            sib_copy(p).wait_recv()
        else:
            for k in range(4):
                pass_copy(k, p).wait_recv()

    def which_pair(turn):
        return pair + turn - 2 * pair * turn

    def shard_rows(turn, piece_at):
        first = 2 * which_pair(turn)
        at = pl.ds(pl.multiple_of(piece_at * cols, 16), cols)
        return jnp.concatenate([bank[first, at], bank[first + 1, at]], axis=0)

    def half_lanes(turn):
        return pl.ds(pl.multiple_of(which_pair(turn) * lanes_half, 128), lanes_half)

    lanes = lax.broadcasted_iota(jnp.int32, (QB, 128), 1) < HD

    def project(turn):
        first = 2 * which_pair(turn)
        at = half_lanes(turn)

        def one(j, _):
            row = pl.ds(1 + j // 2, 1)
            shift = jnp.concatenate([small[first + i, row, 0:cols] for i in range(2)], axis=1)
            value = dot_nt(xq[...], shard_rows(turn, j)) + jnp.where(j == 1, 0.0, shift)
            qkv[pl.ds(pl.multiple_of(j * tokens, QB), tokens), at] = value.astype(BF16)
            return 0

        lax.fori_loop(0, 3, one, 0)

    def attention(turn, row):
        half = which_pair(turn)
        base = pl.multiple_of(row * length, length)
        spot = pl.multiple_of(row * heads * length, length)
        jobs = [(k, b, head) for k in range(heads) for b in range(len(wins)) for head in range(2)]

        def lane(k):
            return pl.ds(pl.multiple_of((half * heads + k) * 128, 128), 128)

        def score(k, b, head):
            first, low, _ = wins[b]
            queries = qkv[pl.ds(base + first, QB), lane(k)].astype(F32) * 0.125
            inside = lanes if head == 0 else jnp.logical_not(lanes)
            chosen = jnp.where(inside, queries, 0.0).astype(BF16)
            return dot_nt(chosen, qkv[pl.ds(tokens + base + low, size), lane(k)]) + bias[row, b]

        def weigh(k, b, head, scores):
            weights = jnp.exp(scores - jnp.max(scores, -1, keepdims=True))
            share = 1.0 / jnp.sum(weights, -1, keepdims=True)
            low_probs = (weights * share).astype(BF16)
            rows = pl.ds(spot + k * length + wins[b][0], QB)
            probs[rows, head * size : (head + 1) * size] = low_probs
            return low_probs

        scores = [score(*job) for job in jobs]
        weights = [weigh(*job, value) for job, value in zip(jobs, scores)]
        results = []
        for (k, b, _), value in zip(jobs, weights):
            rows = pl.ds(2 * tokens + base + wins[b][1], size)
            results.append(dot_nn(value, qkv[rows, lane(k)]))
        for n in range(0, len(jobs), 2):
            k, b, _ = jobs[n]
            rows = pl.ds(base + wins[b][0], QB)
            coded, squash = quantize(jnp.where(lanes, results[n], results[n + 1]), ranges[1])
            cq[rows, lane(k)] = coded.astype(BF16)
            cs[rows, lane(k)] = (1.0 - squash * squash).astype(BF16)
        p_copy(turn, row).start()

    def p_copy(turn, row):
        spot = pl.multiple_of(row * heads * length, length)
        return pltpu.make_async_copy(
            probs.at[pl.ds(spot, heads * length)],
            p_out.at[row * 2 + which_pair(turn)],
            p_sem.at[row],
        )

    def one_turn(turn, _):
        @pl.when(turn == 0)
        def _():
            for p in range(3):
                arrived(True, p)

        @pl.when(turn == 1)
        def _():
            for p in range(3):
                arrived(False, p)

        project(turn)
        pl.when(turn == 0)(lambda: far_step(0))

        @pl.when(turn == 1)
        def _():
            far_step(4)
            last_step(3)

        def one_row(row, _):
            pl.when(turn == 1)(lambda: p_copy(0, row).wait())
            attention(turn, row)
            for at_turn, at_row, steps in (
                (0, 0, lambda: far_step(1, 2)),
                (0, 1, lambda: side_step(0)),
                (1, 0, lambda: [far_step(5, 6), side_step(3)] and None),
                (1, 1, lambda: [far_step(7), side_step(4)] and None),
            ):
                pl.when(jnp.logical_and(turn == at_turn, row == at_row))(steps)
            return 0

        lax.fori_loop(0, rows_here, one_row, 0)

        @pl.when(turn == 0)
        def _():
            arrived(True, 3)

            def own_attn(b, _):
                rows = pl.ds(pl.multiple_of(b * 2 * QB, QB), 2 * QB)
                total[rows] = dot_nn(cq[rows, half_lanes(0)], shard_rows(0, 3))
                return 0

            lax.fori_loop(0, blocks // 2, own_attn, 0)
            side_step(1)
            far_step(3)
            side_step(2)
            last_step(0, 1, 2)

        return 0

    lax.fori_loop(0, 2, one_turn, 0)
    qkv_puts = [
        put(qkv.at[j * tokens : (j + 1) * tokens], ref) for j, ref in enumerate((q_out, k_out, v_out))
    ]
    put(cq, cq_out)
    put(cs, cs_out)
    arrived(False, 3)

    def norm_block(b, _):
        rows = pl.ds(pl.multiple_of(b * QB, QB), QB)
        attn = total[rows] + dot_nn(cq[rows, half_lanes(1)], shard_rows(1, 3))
        normed, inverse = norm(x[rows] + (attn + shifts[0:1]))
        xh[rows] = normed
        inv[rows] = jnp.broadcast_to(inverse, (QB, 128))
        nq[rows] = quantize(normed * gains[0:1] + shifts[1:2], ranges[2])[0].astype(BF16)
        pl.when(b == 0)(lambda: far_step(8))
        pl.when(b == 1)(lambda: side_step(5))
        pl.when(b == 2)(lambda: side_step(6))
        pl.when(b == 3)(lambda: far_step(9))
        return 0

    lax.fori_loop(0, blocks, norm_block, 0)
    xh_put = put(xh, xh_out)
    put(inv, inv_out)
    nq_put = put(nq, nq_out)
    cot_load = load(6, cot_hbm.at[mine], x)

    for row in range(rows_here):
        p_copy(1, row).wait()
    for copy in qkv_puts:
        copy.wait()

    def spread(i, begin, count):
        shard = (2 * pair + i) % 4
        shift = small[shard, 0:1, 0:hidden]
        places = [pl.multiple_of((begin + b) * QB, QB) for b in range(count)]
        pres = [dot_nn(nq[pl.ds(at, QB)], bank[shard, feed_1:feed_2]) + shift for at in places]
        codes = []
        for at, pre in zip(places, pres):
            cdf = 0.5 * (1.0 + lax.erf(pre * ROOT_HALF))
            coded, squash = quantize(pre * cdf, ranges[3])
            slope = cdf + pre * jnp.exp(-0.5 * pre * pre) * INV_ROOT_TWO_PI
            coded = coded.astype(BF16)
            rows = pl.ds(i % 3 * tokens + at, QB)
            probs[rows] = ((1.0 - squash * squash) * slope).astype(BF16)
            qkv[rows] = coded
            codes.append(coded)
        return codes

    def put_slopes(i):
        at = i % 3 * tokens
        return put(probs.at[at : at + tokens], factor_out.at[i])

    def gather(i, code):
        shard = (2 * pair + i) % 4
        return dot_nn(code, bank[shard, feed_2 : feed_2 + hidden])

    for p in range(4, pieces):
        arrived(True, p)
    put(bank.at[flip(t, 1)], bank_out.at[flip(t, 1)])
    slope_puts, code_puts = [], []

    half_way = blocks // 2
    flat[0:tokens] = jnp.zeros((tokens, width), F32)
    slope_puts, code_puts = [], []

    def own_part(n, _):
        i, begin = n // 2, n % 2 * half_way
        for b, code in enumerate(spread(i, begin, half_way)):
            flat[pl.ds(pl.multiple_of((begin + b) * QB, QB), QB)] += gather(i, code)

        @pl.when(n == 0)
        def _():
            far_step(10)
            side_step(7)
            last_step(4)

        @pl.when(n == 1)
        def _():
            far_step(11)
            side_step(8)
            last_step(5)

        @pl.when(n == 2)
        def _():
            side_step(9)
            last_step(6, 7)

        return 0

    lax.fori_loop(0, 4, own_part, 0)
    side_step(10, 11)
    last_step(8, 11)
    for i in range(2):
        slope_puts.append(put_slopes(i))
        code_puts.append(put(qkv.at[i * tokens : (i + 1) * tokens], gq_out.at[i]))
    for p in range(4, 8):
        arrived(False, p)
    for i in range(2):
        shard = (2 * pair + 2 + i) % 4
        put(bank.at[shard, 0:feed_2], bank_out.at[shard, 0:feed_2])
    slope_puts[0].wait()
    code_puts[0].wait()

    def other_part(n, _):
        spread(2 + n // 2, n % 2 * half_way, half_way)
        pl.when(n == 1)(lambda: last_step(9))
        return 0

    lax.fori_loop(0, 4, other_part, 0)
    put_slopes(2)
    put_slopes(3)
    last_step(10)
    for p in range(8, pieces):
        arrived(False, p)
    for i in range(2):
        shard = (2 * pair + 2 + i) % 4
        put(bank.at[shard, feed_2 : feed_2 + hidden], bank_out.at[shard, feed_2 : feed_2 + hidden])
    def close(n, _):
        for b in range(2):
            at = pl.multiple_of((2 * n + b) * QB, QB)
            found = [qkv[pl.ds(i % 3 * tokens + at, QB)] for i in (2, 3)]
            flat[pl.ds(tokens + at, QB)] = gather(2, found[0]) + gather(3, found[1])
        return 0

    lax.fori_loop(0, half_way, close, 0)

    cot_load.wait()
    xq_put.wait()
    xh_put.wait()
    nq_put.wait()
    sums_out[...] = jnp.zeros_like(sums_out)

    def ends(b):
        rows = pl.ds(pl.multiple_of(b * QB, QB), QB)
        there = pl.ds(pl.multiple_of(c * tokens + b * QB, QB), QB)
        local = [
            pltpu.make_async_copy(src.at[rows], dst, end_sem.at[k, b])
            for k, (src, dst) in enumerate(
                ((xq, lo_out.at[there]), (total, dh2_out.at[rows]), (nq, do_out.at[rows]))
            )
        ]
        remote = pltpu.make_async_remote_copy(
            src_ref=xq.at[rows], dst_ref=lo_out.at[there], send_sem=lo_s.at[b], recv_sem=lo_r.at[b],
            device_id=sib, device_id_type=MESH,
        )
        return local + [remote]

    def last_block(b, _):
        rows = pl.ds(pl.multiple_of(b * QB, QB), QB)
        first = xh[rows] * gains[0:1] + shifts[1:2]
        feed = flat[rows] + flat[pl.ds(pl.multiple_of(tokens + b * QB, QB), QB)]
        normed, inverse = norm(first + (feed + shifts[2:3]))
        xq[rows] = (normed * gains[1:2] + shifts[3:4]).astype(BF16)
        grad = x[rows]
        back = norm_back(grad * gains[1:2], normed, inverse)
        total[rows] = back
        nq[rows] = back.astype(BF16)
        for copy in ends(b):
            copy.start()
        sums_out[1:2] += jnp.sum(grad * normed, 0, keepdims=True)
        sums_out[4:5] += jnp.sum(back, 0, keepdims=True)
        sums_out[5:6] += jnp.sum(grad, 0, keepdims=True)
        return 0

    lax.fori_loop(0, blocks, last_block, 0)

    def sent(p, _):
        far_copy(p).wait_send()
        sib_copy(p).wait_send()
        side_copy(p).wait_send()
        inner_copy(p).wait_send()
        for k in range(4):
            pass_copy(k, p).wait_send()
        return 0

    lax.fori_loop(0, pieces, sent, 0)
    for p in range(pieces):
        (direct_copy(p) if p in DIRECT else last_copy(p)).wait_send()
    waited = [xq_put, xh_put, nq_put] + qkv_puts + [slope_puts[0], code_puts[0]]
    for copy in outs:
        if not any(copy is other_copy for other_copy in waited):
            copy.wait()
    for b in range(blocks):
        for copy in ends(b):
            copy.wait()


def forward(inputs, segment_ids, w_qkv, b_qv, w_out, w_ff1, b_ff1, w_ff2, gains, shifts, ranges, cotangent):
    cols, width = w_out.shape
    hidden = w_ff1.shape[1]
    rows, length = segment_ids.shape
    tokens = inputs.shape[0] // 2
    size = windows(length)[0][2]
    bank_rows = 4 * cols + width + hidden
    pieces = bank_rows // cols
    dma = pltpu.SemaphoreType.DMA
    low = lambda *shape: pltpu.VMEM(shape, BF16)
    full = lambda *shape: pltpu.VMEM(shape, F32)
    wide = S((tokens, width), BF16)
    deep = S((tokens, width), F32)
    return pl.pallas_call(
        forward_kernel,
        out_shape=(
            S((4, bank_rows, width), BF16),
            S((6,), F32),
            wide, wide, wide, wide, wide,
            S((rows, width // 256 * length, 2 * size), BF16),
            wide, wide, wide, deep,
            S((tokens, 128), F32),
            S((2 * tokens, width), BF16),
            S((2, tokens, hidden), BF16),
            S((4, tokens, hidden), BF16),
            deep, wide,
            S((8, width), F32),
        ),
        in_specs=[ANY] * 4 + [VMEM] * 2 + [ANY] * 2 + [VMEM] * 3 + [SMEM],
        out_specs=(ANY, SMEM) + (ANY,) * 16 + (VMEM,),
        scratch_shapes=[
            low(4, bank_rows, width),
            full(max(bank_rows, 2 * tokens), width),
            full(tokens, width),
            low(tokens, width),
            low(tokens, width),
            low(3 * tokens, width),
            low(max(rows // 2 * (width // 256) * length, 3 * tokens), 2 * size),
            low(tokens, width),
            low(tokens, width),
            full(tokens, width),
            full(tokens // length, length // QB, QB, size),
            full(tokens, width),
            low(tokens, width),
            full(tokens, 128),
            full(4, 8, width),
            full(2, 8, width),
            dma((7,)), dma((24,)), dma((rows // 2,)), dma((3, tokens // QB)),
            dma((tokens // QB,)), dma((tokens // QB,)), dma((3,)), dma((3,)),
            *[dma((pieces,))] * 12,
            dma((4, pieces)), dma((4, pieces)),
        ],
        compiler_params=pltpu.CompilerParams(
            collective_id=1, has_side_effects=True, vmem_limit_bytes=62 * MIB
        ),
        name="forward",
    )(
        jnp.swapaxes(w_qkv, 1, 2), w_out, w_ff1, w_ff2, b_qv, b_ff1, inputs, cotangent,
        segment_ids, gains, shifts, ranges,
    )


GROUP = 192
QUARTER = GROUP // 4
HOPS = ("core", "y", "z1", "z2", "z3", "ag")
LINE_HOPS = ("zs1", "zs2", "zy", "zb1", "zb2", "zb3")


def sum_scratch(groups, width, extra, small_shape):
    count = max(extra, 1)
    dma = pltpu.SemaphoreType.DMA
    buf = lambda *shape: pltpu.VMEM(shape + (width,), BF16)
    kinds = dict(
        own=buf(groups * GROUP), got_y=buf(groups, QUARTER), part=buf(groups, QUARTER),
        got_1=buf(groups, QUARTER), got_2=buf(groups, QUARTER), got_x=buf(count, 2, QUARTER),
        line_1=buf(groups, 2, QUARTER), line_2=buf(groups, 2, QUARTER), line_y=buf(groups, 2, QUARTER),
        line_x=buf(count, 2, 2, QUARTER),
        small_own=pltpu.VMEM(small_shape, F32), small_got=pltpu.VMEM((5 + extra,) + small_shape, F32),
        x_s=dma((count, groups)), x_r=dma((count, groups)),
        lx_s=dma((count, groups, 2)), lx_r=dma((count, groups, 2)),
        small_s=dma((5 + extra,)), small_r=dma((5 + extra,)),
    )
    for hop in HOPS:
        kinds[hop + "_s"], kinds[hop + "_r"] = dma((groups,)), dma((groups,))
    for hop in LINE_HOPS:
        kinds[hop + "_s"], kinds[hop + "_r"] = dma((groups, 2)), dma((groups, 2))
    return list(kinds), list(kinds.values())


TICKS = (
    ((0, 1),),
    ((0, 0), (0, 3), (0, 2), (1, 1)),
    ((1, 0),),
    ((2, 1),),
    ((1, 3),),
    ((3, 1), (2, 0), (0, 7), (0, 5), (1, 2), (0, 6)),
    ((2, 3), (0, 4), (1, 5), (4, 1)),
    ((3, 0), (2, 2)),
    ((3, 3), (1, 6), (5, 1)),
    ((2, 5), (4, 0)),
    ((3, 2), (1, 4), (0, 8), (4, 3)),
    ((2, 6),),
    ((3, 5), (5, 0), (1, 8)),
    ((4, 2),),
    ((5, 3), (2, 4)),
    ((3, 6), (1, 7), (4, 5)),
    ((2, 8), (5, 2)),
    (
        (0, 11), (3, 4), (4, 6), (2, 7), (5, 5), (6, 1), (6, 0), (0, 10),
        (1, 11), (3, 8), (0, 9), (1, 10), (4, 4),
    ),
    ((2, 11), (3, 7), (5, 6)),
    ((4, 8), (1, 9)),
    ((5, 4), (2, 10)),
    ((3, 11), (4, 7)),
    (),
    ((2, 9), (5, 8)),
    ((4, 11), (6, 5), (3, 10), (5, 7)),
    (),
    (
        (5, 11), (3, 9), (4, 10), (6, 11), (4, 9), (5, 10), (6, 7), (6, 4),
        (6, 3), (6, 6), (5, 9), (6, 2), (6, 10), (6, 8), (6, 9),
    ),
)


class GradientSum:
    def __init__(self, extra, mine, theirs, result, refs):
        self.__dict__.update(refs)
        self.extra, self.mine, self.theirs, self.result = extra, mine, theirs, result
        t, d = lax.axis_index("tensor"), lax.axis_index("dp")
        self.y = d % 2
        self.z = (d // 2) % 4
        self.end = jnp.logical_or(self.z == 0, self.z == 3)
        self.middle = jnp.logical_not(self.end)
        self.sib = (d, flip(t, 1))
        self.side = (flip(d, 1), t)
        self.inner = (flip(d, 2), t)
        self.across = (d + 2 * (3 - 2 * self.z), t)
        self.others = [(flip(d, 8 << b), t) for b in range(extra)]
        self.beyond = [self.across] + self.others
        self.groups = self.own.shape[0] // GROUP

    def announce(self):
        barrier = pltpu.get_barrier_semaphore()

        def tell(peers):
            for peer in peers:
                pl.semaphore_signal(barrier, inc=1, device_id=peer, device_id_type=MESH)

        tell([self.sib, self.side, self.inner])
        pl.when(self.middle)(lambda: tell(self.beyond))

    def meet(self):
        barrier = pltpu.get_barrier_semaphore()
        pl.when(self.end)(lambda: pl.semaphore_wait(barrier, 3))
        pl.when(self.middle)(lambda: pl.semaphore_wait(barrier, 3 + len(self.beyond)))

    def remote(self, src, dst, hop, at, to):
        return pltpu.make_async_remote_copy(
            src_ref=src, dst_ref=dst, send_sem=getattr(self, hop + "_s").at[at],
            recv_sem=getattr(self, hop + "_r").at[at], device_id=to, device_id_type=MESH,
        )

    def small(self, i, to):
        return self.remote(self.small_own, self.small_got.at[i], "small", i, to)

    def small_add(self, i, to):
        self.small(i, to).wait()
        self.small_own[...] = self.small_own[...] + self.small_got[i]

    def small_step(self, step):
        if step == 0:
            self.small(0, self.sib).start()
        if step == 1:
            self.small_add(0, self.sib)
            self.small(1, self.side).start()
        if step == 2:
            self.small_add(1, self.side)
            pl.when(self.end)(lambda: self.small(2, self.inner).start())
        if step == 3:

            def inward():
                self.small(2, self.inner).wait_recv()
                self.small_own[...] = self.small_own[...] + self.small_got[2]
                self.small(3, self.across).start()

            pl.when(self.middle)(inward)
        if step == 4:

            def outward():
                self.small_add(3, self.across)
                for b, peer in enumerate(self.others):
                    self.small(5 + b, peer).start()
                    self.small_add(5 + b, peer)
                self.small(4, self.inner).start()

            pl.when(self.middle)(outward)
        if step == 5:

            def received():
                self.small(2, self.inner).wait_send()
                self.small(4, self.inner).wait_recv()
                self.small_own[...] = self.small_got[4]

            pl.when(self.end)(received)
            pl.when(self.middle)(lambda: self.small(4, self.inner).wait_send())

    def span(self, g):
        return pl.ds(pl.multiple_of(g * GROUP, 16), GROUP)

    def half(self, g, which):
        return pl.ds(pl.multiple_of(g * GROUP + which * QUARTER, 16), QUARTER)

    def line(self, g, i):
        return pl.ds(pl.multiple_of(g * GROUP + (2 + i) * QUARTER, 16), QUARTER)

    def core(self, g):
        return self.remote(self.theirs.at[self.span(g)], self.own.at[self.span(g)], "core", g, self.sib)

    def hop(self, name, g):
        if name == "y":
            return self.remote(self.own.at[self.half(g, 1 - self.y)], self.got_y.at[g], "y", g, self.side)
        if name == "z1":
            return self.remote(self.part.at[g], self.got_1.at[g], "z1", g, self.inner)
        if name == "z2":
            return self.remote(self.part.at[g], self.got_2.at[g], "z2", g, self.across)
        there = self.result.at[self.half(g, self.y)]
        return self.remote(there, there, name, g, self.inner if name == "z3" else self.side)

    def line_hop(self, name, g, i):
        mine = self.own.at[self.line(g, i)]
        if name == "zs1":
            return self.remote(mine, self.line_1.at[g, i], name, (g, i), self.inner)
        if name == "zs2":
            return self.remote(mine, self.line_2.at[g, i], name, (g, i), self.across)
        if name == "zy":
            return self.remote(mine, self.line_y.at[g, i], name, (g, i), self.side)
        there = self.result.at[self.line(g, i)]
        return self.remote(there, there, name, (g, i), self.across if name == "zb2" else self.inner)

    def stage(self, s, g):
        add = lambda a, b: (a.astype(F32) + b.astype(F32)).astype(BF16)
        when = lambda condition, body: pl.when(condition)(body)
        root = [self.z == 1, self.z == 2]
        passer = [self.z == 2, self.z == 1]
        near = [self.z == 0, self.z == 3]
        far = [self.z == 3, self.z == 0]
        if s == 0:
            self.core(g).start()
        if s == 1:
            self.core(g).wait()

            def add_rows(n, _):
                rows = pl.ds(pl.multiple_of(g * GROUP + n * QUARTER, 16), QUARTER)
                self.own[rows] = add(self.own[rows], self.mine[rows])
                return 0

            lax.fori_loop(0, 4, add_rows, 0)
            self.hop("y", g).start()
            when(self.end, lambda: [self.line_hop("zs1", g, i).start() for i in range(2)] and None)
        if s == 2:
            self.hop("y", g).wait()
            self.part[g] = add(self.own[self.half(g, self.y)], self.got_y[g])
            when(self.end, lambda: self.hop("z1", g).start())
            for i in range(2):

                def gather(i=i):
                    self.line_hop("zs1", g, i).wait_recv()
                    rows = self.line(g, i)
                    self.own[rows] = add(self.own[rows], self.line_1[g, i])
                    when(passer[i], lambda: self.line_hop("zs2", g, i).start())

                when(self.middle, gather)
        if s == 3:

            def middle():
                self.hop("z1", g).wait_recv()
                self.part[g] = add(self.part[g], self.got_1[g])
                self.hop("z2", g).start()

            when(self.middle, middle)
            for i in range(2):

                def at_root(i=i):
                    self.line_hop("zs2", g, i).wait_recv()
                    rows = self.line(g, i)
                    self.own[rows] = add(self.own[rows], self.line_2[g, i])
                    self.line_hop("zy", g, i).start()

                when(root[i], at_root)
        if s == 4:

            def total():
                self.hop("z2", g).wait()
                self.part[g] = add(self.part[g], self.got_2[g])
                for b in range(self.extra):
                    copy = self.remote(self.part.at[g], self.got_x.at[b, g % 2], "x", (b, g), self.others[b])
                    copy.start()
                    copy.wait()
                    self.part[g] = add(self.part[g], self.got_x[b, g % 2])
                self.result[self.half(g, self.y)] = self.part[g]
                self.hop("ag", g).start()
                self.hop("z3", g).start()

            when(self.middle, total)
            for i in range(2):

                def spread(i=i):
                    self.line_hop("zy", g, i).wait()
                    rows = self.line(g, i)
                    self.own[rows] = add(self.own[rows], self.line_y[g, i])
                    for b in range(self.extra):
                        copy = self.remote(
                            self.own.at[rows], self.line_x.at[b, g % 2, i], "lx", (b, g, i), self.others[b]
                        )
                        copy.start()
                        copy.wait()
                        self.own[rows] = add(self.own[rows], self.line_x[b, g % 2, i])
                    self.result[rows] = self.own[rows]
                    self.line_hop("zb2", g, i).start()
                    self.line_hop("zb1", g, i).start()

                when(root[i], spread)
        if s == 5:

            def outer():
                self.hop("z3", g).wait_recv()
                self.hop("ag", g).start()

            when(self.end, outer)
            for i in range(2):

                def onward(i=i):
                    self.line_hop("zb2", g, i).wait_recv()
                    self.line_hop("zb3", g, i).start()

                when(passer[i], onward)
        if s == 6:
            self.hop("ag", g).wait()
            for i in range(2):
                when(near[i], lambda i=i: self.line_hop("zb1", g, i).wait_recv())
                when(far[i], lambda i=i: self.line_hop("zb3", g, i).wait_recv())

                def sent_root(i=i):
                    self.line_hop("zb1", g, i).wait_send()
                    self.line_hop("zb2", g, i).wait_send()

                def sent_passer(i=i):
                    self.line_hop("zs2", g, i).wait_send()
                    self.line_hop("zb3", g, i).wait_send()

                when(root[i], sent_root)
                when(passer[i], sent_passer)

            def sent_end():
                self.hop("z1", g).wait_send()
                for i in range(2):
                    self.line_hop("zs1", g, i).wait_send()

            when(self.end, sent_end)
            when(self.middle, lambda: self.hop("z3", g).wait_send())

    def run(self, events):
        for stage, group in events:
            self.stage(stage, group)


def back_kernel(
    extra, names,
    do_hbm, gq_hbm, factor_hbm, nq_hbm, bank, dh2_hbm, xh_hbm, inv_hbm, sums_ref,
    cs_hbm, cq_hbm, q_hbm, k_hbm, v_hbm, p_hbm, xq_hbm, xs_hbm, gains, shifts, ranges,
    g2_out, g1_out, go_out, gq_out, gains_out, shifts_out, bqv_out, bff1_out, dx_full,
    result, inv, grads, do, weights, gq, factor, nq, low, total, dh, xh, wo, cq, dproj, sem, dx_send, dx_recv,
    *refs,
):
    t, d = lax.axis_index("tensor"), lax.axis_index("dp")
    c, pair = t % 2, t // 2
    engine = GradientSum(extra, grads.at[c], grads.at[1 - c], result, dict(zip(names, refs)))
    tokens, width = do.shape
    hidden = gq_hbm.shape[2]
    side = width // 2
    cols = side // 2
    heads = width // 128 // 2
    length = p_hbm.shape[1] // heads
    wins = windows(length)
    size = wins[0][2]
    blocks = tokens // QB
    slots = factor.shape[0] // length

    def load(i, src, dst):
        copy = pltpu.make_async_copy(src, dst, sem.at[i])
        copy.start()
        return copy

    def shard_at(i):
        return (2 * pair + i) % 4

    def load_codes(begin, end, sems):
        return [
            load(sems[i], gq_hbm.at[i, :, begin:end], gq.at[i * tokens : (i + 1) * tokens, begin:end])
            for i in range(2)
        ]

    half_way = hidden // 2
    first_loads = [load(0, do_hbm, do)] + load_codes(0, half_way, (1, 2))

    def load_pair(base):
        copies = []
        for i in range(2):
            s = shard_at(base + i)
            at = pl.ds(i * tokens, tokens)
            for j in range(2):
                spot = weights.at[(2 * j + i) * width : (2 * j + i + 1) * width]
                copies.append(load(3 + 2 * j + i, bank.at[s, 4 * cols + j * width : 4 * cols + (j + 1) * width], spot))
            copies.append(load(7 + i, factor_hbm.at[base + i], factor.at[at]))
        return copies

    engine.announce()
    at = pl.ds(pl.multiple_of(c * tokens, 256), tokens)
    engine.small_own[...] = jnp.zeros_like(engine.small_own)
    engine.small_own[0:8] = sums_ref[...]

    def tick(point):
        engine.run(TICKS[point])

    for copy in first_loads:
        copy.wait()
    code_loads = load_codes(half_way, hidden, (12, 14))
    pair_loads = load_pair(0)

    def weights_2(n, _):
        part, i = n // 2, n % 2
        lanes = pl.ds(pl.multiple_of(part * half_way, 128), half_way)
        value = dot_tn(gq[pl.ds(pl.multiple_of(i * tokens, QB), tokens), lanes], do[...])
        grads[i, pl.ds(pl.multiple_of(part * half_way, 16), half_way)] = value.astype(BF16)

        @pl.when(n == 1)
        def _():
            engine.meet()
            tick(0)
            for copy in code_loads:
                copy.wait()

        return 0

    lax.fori_loop(0, 4, weights_2, 0)
    tick(1)
    for copy in pair_loads:
        copy.wait()
    nq_load = load(9, nq_hbm, nq)
    norm_loads = [load(10, dh2_hbm, dh), load(11, xh_hbm, xh), load(15, inv_hbm, inv)]

    def feed_blocks(own, first, second):
        def one(n, _):
            places = [pl.multiple_of((2 * n + b) * QB, QB) for b in range(2)]
            backs = [
                [
                    dot_nt(do[pl.ds(at, QB)], weights[(2 + i) * width : (3 + i) * width])
                    for i in range(2)
                ]
                for at in places
            ]
            lows = []
            for at, pairs in zip(places, backs):
                lows.append([])
                for i in range(2):
                    spot = pl.ds(i * tokens + at, QB)
                    value = pairs[i] * factor[spot].astype(F32)
                    short = value.astype(BF16)
                    if own:
                        engine.small_own[6 + i : 7 + i] += jnp.sum(value, 0, keepdims=True)
                        low[spot] = short
                    lows[-1].append(short)
            for at, (one_low, two_low) in zip(places, lows):
                rows = pl.ds(at, QB)
                part = dot_nt(one_low, weights[0:width]) + dot_nt(two_low, weights[width : 2 * width])
                total[rows] = part if own else total[rows] + part
            pl.when(n == 0)(functools.partial(tick, first))
            return 0

        lax.fori_loop(0, blocks // 2, one, 0)
        if second is not None:
            tick(second)

    feed_blocks(True, 2, 3)
    pair_loads = load_pair(2)
    nq_load.wait()

    def weights_1(i, _):
        part = dot_tn(nq[...], low[pl.ds(pl.multiple_of(i * tokens, QB), tokens)])
        grads[i, hidden : 2 * hidden] = part.astype(BF16)
        pl.when(i == 0)(functools.partial(tick, 4))
        return 0

    lax.fori_loop(0, 2, weights_1, 0)
    tick(5)
    for copy in pair_loads:
        copy.wait()
    wo_loads = [
        load(27 + s, bank.at[s, 3 * cols : 4 * cols], wo.at[s * cols : (s + 1) * cols]) for s in range(4)
    ]
    mine = pl.ds(pl.multiple_of(pair * side, 128), side)
    cq_load = load(13, cq_hbm.at[:, mine], cq)
    cs_load = load(9, cs_hbm, nq)
    feed_blocks(False, 6, None)
    qkv_loads = [
        load(18 + j, src, weights.at[j * tokens : (j + 1) * tokens])
        for j, src in enumerate((q_hbm, k_hbm, v_hbm))
    ]

    def unit_at(own, u):
        return u // heads, u % heads

    def probs_load(own, u):
        row, which = unit_at(own, u)
        slot = u % slots
        return pltpu.make_async_copy(
            p_hbm.at[row * 2 + (pair if own else 1 - pair), pl.ds(pl.multiple_of(which * length, length), length)],
            factor.at[pl.ds(pl.multiple_of(slot * length, length), length)],
            sem.at[22 + slot],
        )

    units = 2 * heads
    for u in range(slots - 1):
        probs_load(True, u).start()
    tick(7)

    for copy in norm_loads:
        copy.wait()
    xq_load = load(17, xq_hbm, low.at[tokens : 2 * tokens])
    wt_loads = [
        load(31 + s, bank.at[s, 0 : 3 * cols], gq.at[3 * s * cols : 3 * (s + 1) * cols]) for s in range(4)
    ]
    xs_load = load(21, xs_hbm, do)

    def norm_block(b, _):
        rows = pl.ds(pl.multiple_of(b * QB, QB), QB)
        normed = xh[rows]
        squash = jnp.tanh((normed * gains[0:1] + shifts[1:2]) * (1.0 / ranges[2]))
        grad = dh[rows] + total[rows] * (1.0 - squash * squash)
        inverse = jnp.max(inv[rows], axis=1, keepdims=True)
        back = norm_back(grad * gains[0:1], normed, inverse)
        dh[rows] = back
        low[rows] = back.astype(BF16)
        engine.small_own[0:1] += jnp.sum(grad * normed, 0, keepdims=True)
        engine.small_own[2:3] += jnp.sum(back, 0, keepdims=True)
        engine.small_own[3:4] += jnp.sum(grad, 0, keepdims=True)
        return 0

    lax.fori_loop(0, blocks, norm_block, 0)
    tick(8)
    for copy in wo_loads:
        copy.wait()
    cq_load.wait()
    cs_load.wait()
    d_attn = low.at[0:tokens]
    part = dot_tn(cq[...], d_attn[...]).astype(BF16)
    for i in range(2):
        grads[i, 2 * hidden : 2 * hidden + cols] = part[i * cols : (i + 1) * cols]
    tick(9)

    def context_block(b, _):
        rows = pl.ds(pl.multiple_of(b * QB, QB), QB)
        nq[rows] = (dot_nt(d_attn[rows], wo[...]) * nq[rows].astype(F32)).astype(BF16)
        return 0

    lax.fori_loop(0, blocks, context_block, 0)
    tick(10)

    for copy in qkv_loads:
        copy.wait()
    lanes = lax.broadcasted_iota(jnp.int32, (QB, 128), 1) < HD

    def attention(own, u):
        row, which = unit_at(own, u)
        probs_load(own, u).wait()

        @pl.when(u + slots - 1 < units)
        def _():
            probs_load(own, u + slots - 1).start()

        half = pair if own else 1 - pair
        lane = pl.ds(pl.multiple_of((half * heads + which) * 128, 128), 128)
        here = pl.ds(pl.multiple_of(which * 128, 128), 128)
        slot = pl.multiple_of((u % slots) * length, length)
        base = pl.multiple_of(row * length, length)
        wide = lax.broadcasted_iota(jnp.int32, (size, 128), 1) < HD
        jobs = [(b, head) for b in range(len(wins)) for head in range(2)]

        def shares(b, head):
            return factor[pl.ds(slot + wins[b][0], QB), head * size : (head + 1) * size]

        def first_product(b, head):
            first, begin, _ = wins[b]
            own_lanes = lanes if head == 0 else jnp.logical_not(lanes)
            context = nq[pl.ds(base + first, QB), lane].astype(F32)
            chosen = jnp.where(own_lanes, context, 0.0).astype(BF16)
            return dot_nt(chosen, weights[pl.ds(2 * tokens + base + begin, size), lane])

        def d_score(b, head, d_probs):
            exact = shares(b, head).astype(F32)
            both = exact * d_probs
            return (both - exact * jnp.sum(both, -1, keepdims=True)).astype(BF16)

        def products(b, head, d_low):
            first, begin, _ = wins[b]
            rows = pl.ds(base + first, QB)
            return (
                dot_nn(d_low, weights[pl.ds(tokens + base + begin, size), lane]),
                dot_tn(d_low, weights[rows, lane]),
                dot_tn(shares(b, head), nq[rows, lane]),
            )

        d_probs = [first_product(*job) for job in jobs]
        d_lows = [d_score(*job, value) for job, value in zip(jobs, d_probs)]
        found = [products(*job, value) for job, value in zip(jobs, d_lows)]
        d_keys, d_values = [], []
        for b, (first, _, _) in enumerate(wins):
            got = found[2 * b : 2 * b + 2]
            rows = pl.ds(base + first, QB)
            dproj[0, rows, here] = (jnp.where(lanes, got[0][0], got[1][0]) * 0.125).astype(BF16)
            d_keys.append(jnp.where(wide, got[0][1], got[1][1]))
            d_values.append(jnp.where(wide, got[0][2], got[1][2]))
        for j, parts, scale in ((1, d_keys, 0.125), (2, d_values, 1.0)):
            for spot in range(0, length, SPAN):
                terms = [
                    part[spot - begin : spot - begin + SPAN]
                    for part, (_, begin, _) in zip(parts, wins)
                    if begin <= spot < begin + size
                ]
                dproj[j, pl.ds(base + spot, SPAN), here] = (sum(terms[1:], terms[0]) * scale).astype(BF16)

    def back_through(own, finish):
        first = 2 * pair if own else 2 - 2 * pair

        def rows(j):
            found = [
                gq[pl.ds(pl.multiple_of(((first + i) * 3 + j) * cols, 16), cols)] for i in range(2)
            ]
            return jnp.concatenate(found, axis=0)

        def block(n, _):
            at = pl.ds(pl.multiple_of(n * QB, QB), QB)
            terms = [dot_nn(dproj[j, at], rows(j)) for j in range(3)]
            finish(at, terms[0] + terms[1] + terms[2])
            return 0

        lax.fori_loop(0, blocks, block, 0)

    def ticks_after(u, first):
        for k in range(units):
            if TICKS[first + k]:
                pl.when(u == k)(functools.partial(tick, first + k))

    def own_unit(u, _):
        attention(True, u)
        ticks_after(u, 11)
        return 0

    lax.fori_loop(0, units, own_unit, 0)
    for u in range(slots - 1):
        probs_load(False, u).start()
    for copy in wt_loads:
        copy.wait()
    xq_load.wait()
    def weights_qkv(j, _):
        part = dot_tn(dproj[j], low[tokens : 2 * tokens]).astype(BF16)
        at = pl.ds(pl.multiple_of(2 * hidden + (j + 1) * cols, 16), cols)
        for i in range(2):
            grads[i, at] = part[i * cols : (i + 1) * cols]
        return 0

    lax.fori_loop(0, 3, weights_qkv, 0)
    engine.small_own[8:9, 0:side] = jnp.sum(dproj[0].astype(F32), 0, keepdims=True)
    engine.small_own[9:10, 0:side] = jnp.sum(dproj[2].astype(F32), 0, keepdims=True)
    tick(17)
    engine.small_step(0)

    def keep(rows, value):
        total[rows] = value

    back_through(True, keep)
    tick(18)

    def other_unit(u, _):
        attention(False, u)
        ticks_after(u, 19)
        for k, step in ((0, 1), (3, 2)):
            pl.when(u == k)(functools.partial(engine.small_step, step))
        return 0

    lax.fori_loop(0, units, other_unit, 0)
    xs_load.wait()

    def results(rows, value):
        factor[rows] = (dh[rows] + (total[rows] + value) * do[rows].astype(F32)).astype(BF16)

    back_through(False, results)
    dx_copy = pltpu.make_async_remote_copy(
        src_ref=factor.at[0:tokens], dst_ref=dx_full.at[at], send_sem=dx_send, recv_sem=dx_recv,
        device_id=engine.sib, device_id_type=MESH,
    )
    dx_copy.start()
    outs = [load(26, factor.at[0:tokens], dx_full.at[at])]
    tick(25)
    engine.small_step(3)

    def small_results():
        engine.small_step(5)
        sums = engine.small_own[...]
        here = sums[:, 0:cols]
        for s in range(1, 4):
            here = jnp.where(t == s, sums[:, s * cols : (s + 1) * cols], here)
        gains_out[...] = here[0:2]
        shifts_out[...] = here[2:6]
        bqv_out[...] = jnp.where(c == 0, sums[8:10, 0:cols], sums[8:10, cols:side])
        bff1_out[...] = jnp.where(c == 0, sums[6:7], sums[7:8]).reshape(hidden)

    leaving = [
        (0, 4, g2_out, 0, hidden),
        (4, 8, g1_out, hidden, 2 * hidden),
        (8, 9, go_out, 2 * hidden, 2 * hidden + cols),
        (9, 12, gq_out, 2 * hidden + cols, 2 * hidden + 4 * cols),
    ]
    complete = {g for events in TICKS[:-1] for s, g in events if s == 6}
    for n, event in enumerate((None,) + TICKS[-1]):
        if n == 4:
            engine.small_step(4)
        if n == 10:
            small_results()
        if event is not None:
            engine.stage(*event)
            if event[0] == 6:
                complete.add(event[1])
        for k, (first, last, ref, begin, end) in enumerate(leaving):
            if ref is not None and complete.issuperset(range(first, last)):
                outs.append(load(k, result.at[begin:end], ref))
                leaving[k] = (first, last, None, begin, end)
    dx_copy.wait()
    for copy in outs:
        copy.wait()


def back(
    nd, do, gq, factor, nq, bank, dh2, xh, inv, sums, cs, cq, q, k, v, probs, xq, xs,
    gains, shifts, ranges,
):
    tokens, width = do.shape
    hidden = gq.shape[2]
    cols = width // 4
    rows = 2 * hidden + 4 * cols
    extra = (nd // 8).bit_length() - 1
    dma = pltpu.SemaphoreType.DMA
    names, scratch = sum_scratch(rows // GROUP, width, extra, (16, width))
    buf = lambda *shape: pltpu.VMEM(shape, BF16)
    return pl.pallas_call(
        functools.partial(back_kernel, extra, names),
        out_shape=(
            S((hidden, width), BF16),
            S((width, hidden), BF16),
            S((cols, width), BF16),
            S((3 * cols, width), BF16),
            S((2, cols), F32),
            S((4, cols), F32),
            S((2, cols), F32),
            S((hidden,), F32),
            S((2 * tokens, width), BF16),
        ),
        in_specs=[ANY] * 8 + [VMEM] + [ANY] * 8 + [VMEM, VMEM, SMEM],
        out_specs=(ANY,) * 4 + (VMEM,) * 4 + (ANY,),
        scratch_shapes=[
            buf(rows, width),
            pltpu.VMEM((tokens, 128), F32),
            buf(2, rows, width),
            buf(tokens, width),
            buf(max(4 * width, 3 * tokens), width),
            buf(max(3 * width, 2 * tokens), width),
            buf(2 * tokens, width),
            buf(tokens, width),
            buf(2 * tokens, width),
            pltpu.VMEM((tokens, width), F32),
            pltpu.VMEM((tokens, width), F32),
            pltpu.VMEM((tokens, width), F32),
            buf(width, width),
            buf(tokens, width // 2),
            buf(3, tokens, width // 2),
            dma((35,)),
            dma,
            dma,
            *scratch,
        ],
        compiler_params=pltpu.CompilerParams(
            collective_id=2, has_side_effects=True, vmem_limit_bytes=62 * MIB
        ),
        name="back",
    )(
        do, gq, factor, nq, bank, dh2, xh, inv, sums, cs, cq, q, k, v, probs, xq, xs,
        gains, shifts, ranges,
    )


def finish_kernel(*refs):
    half = len(refs) // 2
    for src, dst in zip(refs[: half - 1], refs[half:-1]):
        dst[...] = src[...].astype(F32)
    for j in range(refs[-1].shape[0]):
        refs[-1][j] = refs[half - 1][j]


def finish(*arrays):
    steps = 8
    specs = []
    for array in arrays[:-1]:
        rows = array.shape[0]
        if array.ndim == 2 and rows % (16 * steps) == 0:
            specs.append(pl.BlockSpec((rows // steps, array.shape[1]), lambda i: (i, 0)))
        elif array.ndim == 2 and rows % (16 * steps // 2) == 0:
            specs.append(pl.BlockSpec((2 * rows // steps, array.shape[1]), lambda i: (i // 2, 0)))
        else:
            specs.append(pl.BlockSpec(array.shape, lambda i, n=array.ndim: (0,) * n))
    specs.append(SMEM)
    return pl.pallas_call(
        finish_kernel,
        out_shape=tuple(S(array.shape, F32) for array in arrays),
        grid=(steps,),
        in_specs=specs,
        out_specs=tuple(specs),
        compiler_params=pltpu.CompilerParams(vmem_limit_bytes=62 * MIB),
        name="finish",
    )(*arrays)


def per_device(
    nd, inputs, segment_ids, w_qkv, b_qv, w_out, w_ff1, b_ff1, w_ff2, norm_gains, shift_biases,
    act_ranges, cotangent,
):
    width = inputs.shape[1]
    cols = w_qkv.shape[2]
    (
        bank, weight_max, xq, xs, q, k, v, probs, cq, cs, nq, xh, inv, layer_out, gq, factor, dh2, do,
        sums,
    ) = forward(
        inputs, segment_ids, w_qkv, b_qv, w_out, w_ff1, b_ff1, w_ff2, norm_gains, shift_biases,
        act_ranges, cotangent,
    )
    (
        grad_ff2, grad_ff1, grad_out, grad_qkv, grad_gains, grad_shifts, grad_bqv, grad_bff1, input_grad,
    ) = back(
        nd, do, gq, factor, nq, bank, dh2, xh, inv, sums, cs, cq, q, k, v, probs, xq, xs,
        norm_gains, shift_biases, act_ranges,
    )
    (
        layer_out, input_grad, grad_ff2, grad_ff1, grad_out, grad_qkv, grad_gains, grad_shifts, grad_bqv,
        grad_bff1, weight_max,
    ) = finish(
        layer_out, input_grad, grad_ff2, grad_ff1, grad_out, grad_qkv, grad_gains, grad_shifts, grad_bqv,
        grad_bff1, weight_max,
    )
    grad_qkv = grad_qkv.reshape(3, cols, width).transpose(0, 2, 1)
    return (
        layer_out, input_grad, grad_qkv, grad_bqv, grad_out, grad_ff1, grad_bff1, grad_ff2,
        grad_gains, grad_shifts, weight_max,
    )


def solution(mesh):
    return jax.shard_map(
        functools.partial(per_device, mesh.shape["dp"]),
        mesh=mesh,
        in_specs=(
            P("dp", None),
            P("dp", None),
            P(None, None, "tensor"),
            P(None, "tensor"),
            P("tensor", None),
            P(None, "tensor"),
            P("tensor"),
            P("tensor", None),
            P(),
            P(),
            P(),
            P("dp", None),
        ),
        out_specs=(
            P("dp", None),
            P("dp", None),
            P(None, None, "tensor"),
            P(None, "tensor"),
            P("tensor", None),
            P(None, "tensor"),
            P("tensor"),
            P("tensor", None),
            P(None, "tensor"),
            P(None, "tensor"),
            P(),
        ),
        check_vma=False,
    )
```

profile of v0, /device:TPU:0, one launch (start us, length us, event | category | flops | bytes accessed | tf_op | source)
XLA Modules:
  0.0 180.2 jit_solution(334339348935820034)
XLA Ops:
  0.6 76.0 %forward.1 = (bf16[4,2304,768]{2,1,0:T(8,128)(2,1)}, f32[6]{0:T(128)}, bf16[1024,768]{1,0:T(8,128)(2,1)}, bf16[1024,768]{1,0:T(8,128)(2,1)}, bf16[1024,768]{1,0:...) custom-call(f32[3,192,768]{2,1,0:T(8,128)} %bitcast.4, ...), custom_call_target="tpu_custom_call" | custom-call | tf_op jit(solution)/shard_map/forward/pallas_call | solution.py:598
  76.7 91.4 %back.1 = (bf16[768,768]{1,0:T(8,128)(2,1)}, bf16[768,768]{1,0:T(8,128)(2,1)}, bf16[192,768]{1,0:T(8,128)(2,1)}, bf16[576,768]{1,0:T(8,128)(2,1)}, f32[2,192]{1,...) custom-call(bf16[1024,768]{1,0:T(8,128)(2,1)} %get-tuple-element.51.do_hbm, ...), custom_call_target="tpu_custom_call" | custom-call | tf_op jit(solution)/shard_map/back/pallas_call | solution.py:1341
  168.1 11.9 %finish.1 = (f32[2048,768]{1,0:T(8,128)}, f32[2048,768]{1,0:T(8,128)}, f32[768,768]{1,0:T(8,128)}, f32[768,768]{1,0:T(8,128)}, f32[192,768]{1,0:T(8,128)}, /*ind...) custom-call(bf16[2048,768]{1,0:T(8,128)(2,1)} %get-tuple-element.50., ...), custom_call_target="tpu_custom_call" | custom-call | tf_op jit(solution)/shard_map/finish/pallas_call | solution.py:1407
where the time goes:
time: 181 us; the launch traced here: 180 us
  Pallas kernels  179 us (99%)
    pallas_call x1, Pallas kernels, back(): pl.pallas_call(functools.partial(back_kernel, extra, names), out_shape=(S...  91.4 us
    pallas_call x1, Pallas kernels, forward(): pl.pallas_call(forward_kernel, out_shape=(S((4, bank_rows, width), BF16),...  76 us
    pallas_call x1, Pallas kernels, finish(): pl.pallas_call(finish_kernel, out_shape=tuple((S(array.shape, F32) for ar...  11.9 us

commit v1 on v0

--- a/solution.py
+++ b/solution.py
@@ -91,7 +91,7 @@
 def forward_kernel(
     wqkv, wout, wff1, wff2, bqv, bff1, x_hbm, cot_hbm, seg_ref, gains, shifts, ranges,
     bank_out, top_out, xq_out, xs_out, q_out, k_out, v_out, p_out, cq_out, cs_out, nq_out, xh_out,
-    inv_out, lo_out, gq_out, factor_out, dh2_out, do_out, sums_out,
+    inv_out, lo_out, gq_out, factor_out, do_out, sums_out,
     bank, flat, x, xq, xs, qkv, probs, cq, cs, total, bias, xh, nq, inv, small, scales,
     sem, out_sem, p_sem, end_sem, lo_s, lo_r, small_s, small_r, sib_s, sib_r, far_s, far_r,
     direct_s, direct_r, side_s, side_r, inner_s, inner_r, last_s, last_r, pass_s, pass_r,
@@ -533,7 +533,7 @@
         local = [
             pltpu.make_async_copy(src.at[rows], dst, end_sem.at[k, b])
             for k, (src, dst) in enumerate(
-                ((xq, lo_out.at[there]), (total, dh2_out.at[rows]), (nq, do_out.at[rows]))
+                ((xq, lo_out.at[there]), (nq, do_out.at[rows]))
             )
         ]
         remote = pltpu.make_async_remote_copy(
@@ -550,7 +550,6 @@
         xq[rows] = (normed * gains[1:2] + shifts[3:4]).astype(BF16)
         grad = x[rows]
         back = norm_back(grad * gains[1:2], normed, inverse)
-        total[rows] = back
         nq[rows] = back.astype(BF16)
         for copy in ends(b):
             copy.start()
@@ -607,11 +606,11 @@
             S((2 * tokens, width), BF16),
             S((2, tokens, hidden), BF16),
             S((4, tokens, hidden), BF16),
-            deep, wide,
+            wide,
             S((8, width), F32),
         ),
         in_specs=[ANY] * 4 + [VMEM] * 2 + [ANY] * 2 + [VMEM] * 3 + [SMEM],
-        out_specs=(ANY, SMEM) + (ANY,) * 16 + (VMEM,),
+        out_specs=(ANY, SMEM) + (ANY,) * 15 + (VMEM,),
         scratch_shapes=[
             low(4, bank_rows, width),
             full(max(bank_rows, 2 * tokens), width),
@@ -952,7 +951,7 @@
 
 def back_kernel(
     extra, names,
-    do_hbm, gq_hbm, factor_hbm, nq_hbm, bank, dh2_hbm, xh_hbm, inv_hbm, sums_ref,
+    do_hbm, gq_hbm, factor_hbm, nq_hbm, bank, xh_hbm, inv_hbm, sums_ref,
     cs_hbm, cq_hbm, q_hbm, k_hbm, v_hbm, p_hbm, xq_hbm, xs_hbm, gains, shifts, ranges,
     g2_out, g1_out, go_out, gq_out, gains_out, shifts_out, bqv_out, bff1_out, dx_full,
     result, inv, grads, do, weights, gq, factor, nq, low, total, dh, xh, wo, cq, dproj, sem, dx_send, dx_recv,
@@ -1033,7 +1032,7 @@
     for copy in pair_loads:
         copy.wait()
     nq_load = load(9, nq_hbm, nq)
-    norm_loads = [load(10, dh2_hbm, dh), load(11, xh_hbm, xh), load(15, inv_hbm, inv)]
+    norm_loads = [load(11, xh_hbm, xh), load(15, inv_hbm, inv)]
 
     def feed_blocks(own, first, second):
         def one(n, _):
@@ -1116,13 +1115,12 @@
     wt_loads = [
         load(31 + s, bank.at[s, 0 : 3 * cols], gq.at[3 * s * cols : 3 * (s + 1) * cols]) for s in range(4)
     ]
-    xs_load = load(21, xs_hbm, do)
 
     def norm_block(b, _):
         rows = pl.ds(pl.multiple_of(b * QB, QB), QB)
         normed = xh[rows]
         squash = jnp.tanh((normed * gains[0:1] + shifts[1:2]) * (1.0 / ranges[2]))
-        grad = dh[rows] + total[rows] * (1.0 - squash * squash)
+        grad = do[rows].astype(F32) + total[rows] * (1.0 - squash * squash)
         inverse = jnp.max(inv[rows], axis=1, keepdims=True)
         back = norm_back(grad * gains[0:1], normed, inverse)
         dh[rows] = back
@@ -1133,6 +1131,7 @@
         return 0
 
     lax.fori_loop(0, blocks, norm_block, 0)
+    xs_load = load(21, xs_hbm, do)
     tick(8)
     for copy in wo_loads:
         copy.wait()
@@ -1327,7 +1326,7 @@
 
 
 def back(
-    nd, do, gq, factor, nq, bank, dh2, xh, inv, sums, cs, cq, q, k, v, probs, xq, xs,
+    nd, do, gq, factor, nq, bank, xh, inv, sums, cs, cq, q, k, v, probs, xq, xs,
     gains, shifts, ranges,
 ):
     tokens, width = do.shape
@@ -1351,7 +1350,7 @@
             S((hidden,), F32),
             S((2 * tokens, width), BF16),
         ),
-        in_specs=[ANY] * 8 + [VMEM] + [ANY] * 8 + [VMEM, VMEM, SMEM],
+        in_specs=[ANY] * 7 + [VMEM] + [ANY] * 8 + [VMEM, VMEM, SMEM],
         out_specs=(ANY,) * 4 + (VMEM,) * 4 + (ANY,),
         scratch_shapes=[
             buf(rows, width),
@@ -1379,7 +1378,7 @@
         ),
         name="back",
     )(
-        do, gq, factor, nq, bank, dh2, xh, inv, sums, cs, cq, q, k, v, probs, xq, xs,
+        do, gq, factor, nq, bank, xh, inv, sums, cs, cq, q, k, v, probs, xq, xs,
         gains, shifts, ranges,
     )
 
@@ -1422,8 +1421,7 @@
     width = inputs.shape[1]
     cols = w_qkv.shape[2]
     (
-        bank, weight_max, xq, xs, q, k, v, probs, cq, cs, nq, xh, inv, layer_out, gq, factor, dh2, do,
-        sums,
+        bank, weight_max, xq, xs, q, k, v, probs, cq, cs, nq, xh, inv, layer_out, gq, factor, do, sums,
     ) = forward(
         inputs, segment_ids, w_qkv, b_qv, w_out, w_ff1, b_ff1, w_ff2, norm_gains, shift_biases,
         act_ranges, cotangent,
@@ -1431,7 +1429,7 @@
     (
         grad_ff2, grad_ff1, grad_out, grad_qkv, grad_gains, grad_shifts, grad_bqv, grad_bff1, input_grad,
     ) = back(
-        nd, do, gq, factor, nq, bank, dh2, xh, inv, sums, cs, cq, q, k, v, probs, xq, xs,
+        nd, do, gq, factor, nq, bank, xh, inv, sums, cs, cq, q, k, v, probs, xq, xs,
         norm_gains, shift_biases, act_ranges,
     )
     (

time: 181 us -> 181 us (level)
  no operation moved by 1% of the time
where the time goes in v1:
time: 181 us; the launch traced here: 180 us
  Pallas kernels  179 us (99%)
    pallas_call x1, Pallas kernels, back(): pl.pallas_call(functools.partial(back_kernel, extra, names), out_shape=(S...  91.5 us
    pallas_call x1, Pallas kernels, forward(): pl.pallas_call(forward_kernel, out_shape=(S((4, bank_rows, width), BF16),...  76 us
    pallas_call x1, Pallas kernels, finish(): pl.pallas_call(finish_kernel, out_shape=tuple((S(array.shape, F32) for ar...  11.9 us

profile of v1, /device:TPU:0, one launch (start us, length us, event | category | flops | bytes accessed | tf_op | source)
XLA Modules:
  0.0 180.2 jit_solution(11692962658766769895)
XLA Ops:
  0.6 76.0 %forward.1 = (bf16[4,2304,768]{2,1,0:T(8,128)(2,1)}, f32[6]{0:T(128)}, bf16[1024,768]{1,0:T(8,128)(2,1)}, bf16[1024,768]{1,0:T(8,128)(2,1)}, bf16[1024,768]{1,0:...) custom-call(f32[3,192,768]{2,1,0:T(8,128)} %bitcast.4, ...), custom_call_target="tpu_custom_call" | custom-call | tf_op jit(solution)/shard_map/forward/pallas_call | solution.py:597
  76.6 91.5 %back.1 = (bf16[768,768]{1,0:T(8,128)(2,1)}, bf16[768,768]{1,0:T(8,128)(2,1)}, bf16[192,768]{1,0:T(8,128)(2,1)}, bf16[576,768]{1,0:T(8,128)(2,1)}, f32[2,192]{1,...) custom-call(bf16[1024,768]{1,0:T(8,128)(2,1)} %get-tuple-element.50.do_hbm, ...), custom_call_target="tpu_custom_call" | custom-call | tf_op jit(solution)/shard_map/back/pallas_call | solution.py:1340
  168.1 11.9 %finish.1 = (f32[2048,768]{1,0:T(8,128)}, f32[2048,768]{1,0:T(8,128)}, f32[768,768]{1,0:T(8,128)}, f32[768,768]{1,0:T(8,128)}, f32[192,768]{1,0:T(8,128)}, /*ind...) custom-call(bf16[2048,768]{1,0:T(8,128)(2,1)} %get-tuple-element.49., ...), custom_call_target="tpu_custom_call" | custom-call | tf_op jit(solution)/shard_map/finish/pallas_call | solution.py:1406
